TPU v7x, 768 devices: a whole 4x8x12 slice. The times are simulated.
768 devices in a mesh: group: 24 (over z, core), expert: 32 (over y, x).
Axes of the slice: x: 4, y: 8, z: 12, core: 2. Of those that a mesh axis runs over, the one named last changes fastest.
Arguments:
- hidden_in: bfloat16 [98304, 1024], P(('group', 'expert')), parts along dimension 0, may hold values from -6 to 6
- out_grad: bfloat16 [98304, 1024], P(('group', 'expert')), parts along dimension 0, may hold values from -6 to 6
- gate_probs: float32 [98304, 2], P(('group', 'expert')), parts along dimension 0, may hold values from 0.25 to 2
- expert_ids: int32 [98304, 2], P(('group', 'expert')), parts along dimension 0, may hold values from 0 to 31, as said below
- w_gate: bfloat16 [32, 1024, 768], P('expert'), may hold values from -0.1875 to 0.1875
- w_up: bfloat16 [32, 1024, 768], P('expert'), may hold values from -0.1875 to 0.1875
- w_down: bfloat16 [32, 768, 1024], P('expert'), may hold values from -0.0546875 to 0.0546875
Outputs:
- input_grad: bfloat16 [98304, 1024], P(('group', 'expert')), parts along dimension 0
- prob_grad: bfloat16 [98304, 2], P(('group', 'expert')), parts along dimension 0
There are 24 independent parts, one for each index of `group`. A program takes and returns all parts, laid end to end along the dimension named above; an argument that names none is the same for every part. Nothing has to cross between parts.
Inputs may be any that keep to these rules, and one draw needn't show every extreme that they name: `expert_ids`: each row names 2 different experts. Among the 128 rows of one device no expert is named more than 16 times, and in every draw one expert is named exactly 16 times by the rows of every device.
All inputs are finite; a program needn't handle non-finite values.
Results may differ from a plain program's by a relative error of at most 0.0057.
Values may be sent and summed in bfloat16 or wider, within the bound.
A program may use at most 32 MiB of HBM per device.

v0:
```python
import jax
import jax.numpy as jnp
from jax import lax
from jax.sharding import PartitionSpec as P

EXPERTS = 32
TOPK = 2
MOST = 16


def forward_part(rows_in, gate_w, up_w):
    gate_pre = jnp.einsum("erd,edf->erf", rows_in, gate_w, preferred_element_type=jnp.float32)
    up_pre = jnp.einsum("erd,edf->erf", rows_in, up_w, preferred_element_type=jnp.float32)
    return (gate_pre, up_pre)


def backward_part(gate_pre, up_pre, rows_grad, gate_w, up_w, down_w):
    sigmoid_a = jax.nn.sigmoid(gate_pre)
    silu_a = gate_pre * sigmoid_a
    hidden = silu_a * up_pre
    hidden_grad = jnp.einsum("erd,efd->erf", rows_grad, down_w, preferred_element_type=jnp.float32)
    prob_rows = jnp.sum(hidden_grad * hidden, axis=-1).astype(jnp.bfloat16)
    gate_grad = (hidden_grad * up_pre * sigmoid_a * (1.0 + gate_pre * (1.0 - sigmoid_a))).astype(
        jnp.bfloat16
    )
    up_grad = (hidden_grad * silu_a).astype(jnp.bfloat16)
    input_rows = jnp.einsum("erf,edf->erd", gate_grad, gate_w, preferred_element_type=jnp.float32)
    input_rows = input_rows + jnp.einsum(
        "erf,edf->erd", up_grad, up_w, preferred_element_type=jnp.float32
    )
    return (input_rows.astype(jnp.bfloat16), prob_rows)


def ranks_of(flat_ids, count):
    onehot = (flat_ids[:, None] == jnp.arange(count, dtype=jnp.int32)[None, :]).astype(jnp.int32)
    slot_rank = jnp.sum((jnp.cumsum(onehot, axis=0) - 1) * onehot, axis=1)
    return slot_rank


def per_device(hidden_in, out_grad, gate_probs, expert_ids, w_gate, w_up, w_down):
    width = hidden_in.shape[1]
    tokens_here = hidden_in.shape[0]
    flat_ids = expert_ids.reshape(-1)
    slot_rank = ranks_of(flat_ids, EXPERTS)
    target = flat_ids * MOST + slot_rank
    token_rows = jnp.arange(flat_ids.shape[0], dtype=jnp.int32) // TOPK
    empty = jnp.zeros((EXPERTS * MOST, width), jnp.bfloat16)
    stash_send = empty.at[target].set(hidden_in[token_rows]).reshape(EXPERTS, MOST, width)
    grad_send = empty.at[target].set(out_grad[token_rows]).reshape(EXPERTS, MOST, width)
    stash_recv, grad_recv = (
        lax.all_to_all(stash_send, "expert", split_axis=0, concat_axis=1, tiled=True),
        lax.all_to_all(grad_send, "expert", split_axis=0, concat_axis=1, tiled=True),
    )
    gate_pre, up_pre = forward_part(stash_recv, w_gate, w_up)
    input_rows, prob_rows = backward_part(gate_pre, up_pre, grad_recv, w_gate, w_up, w_down)
    input_back, prob_back = (
        lax.all_to_all(input_rows, "expert", split_axis=1, concat_axis=0, tiled=True),
        lax.all_to_all(prob_rows, "expert", split_axis=1, concat_axis=0, tiled=True),
    )
    picked = input_back.reshape(EXPERTS * MOST, width)[target].reshape(tokens_here, TOPK, width)
    input_grad = jnp.sum(picked.astype(jnp.float32) * gate_probs[:, :, None], axis=1).astype(
        jnp.bfloat16
    )
    prob_grad = prob_back.reshape(-1)[target].reshape(tokens_here, TOPK)
    return (input_grad, prob_grad)


def solution(mesh):
    in_specs = (
        P(("group", "expert"), None),
        P(("group", "expert"), None),
        P(("group", "expert"), None),
        P(("group", "expert"), None),
        P("expert", None, None),
        P("expert", None, None),
        P("expert", None, None),
    )
    out_specs = (P(("group", "expert"), None), P(("group", "expert"), None))
    return jax.shard_map(
        per_device, mesh=mesh, in_specs=in_specs, out_specs=out_specs, check_vma=False
    )
```

profile of v0, /device:TPU:324, one launch (start us, length us, event | category | flops | bytes accessed | tf_op | source)
XLA Modules:
  0.0 155.1 jit_solution(7611408555360230847)
XLA Ops:
  0.6 0.9 copy.25
  3.7 5.3 %scatter_custom_fusion.1 = bf16[512,1024]{1,0:T(8,128)(2,1)} fusion(s32[256]{0:T(256)S(1)} %bitcast.56, bf16[128,1024]{1,0:T(8,128)(2,1)} %param.7, s32[1024]{0:T(1024)S(1)} %pad_clamp_fusion.1, bf16[]{:T(256)} %constant.27.clone.1), kind=kCustom, calls=%fused_computation.25 | custom fusion | bytes 1049088 | tf_op jit(solution)/shard_map/scatter | solution.py:48
  9.0 10.2 %all-to-all-start.1 = ((bf16[32,16,1024]{2,1,0:T(8,128)(2,1)}), bf16[32,16,1024]{2,1,0:T(8,128)(2,1)S(1)}, u32[]{:S(2)}, u32[]{:S(2)}) async-start(bf16[32,16,1024]{2,1,0:T(8,128)(2,1)} %bitcast.7), calls=%async_computation.1 | async-start | bytes 2097152 | tf_op jit(solution)/shard_map/all_to_all | solution.py:51
  19.3 5.3 %scatter_custom_fusion = bf16[512,1024]{1,0:T(8,128)(2,1)} fusion(s32[256]{0:T(256)S(1)} %bitcast.57, bf16[128,1024]{1,0:T(8,128)(2,1)} %param.8, s32[1024]{0:T(1024)S(1)} %pad_clamp_fusion.1, bf16[]{:T(256)} %constant.27.clone.1), kind=kCustom, calls=%fused_computation.27 | custom fusion | bytes 1049088 | tf_op jit(solution)/shard_map/scatter | solution.py:49
  24.5 22.8 %all-to-all-done.1 = bf16[32,16,1024]{2,1,0:T(8,128)(2,1)S(1)} async-done(((bf16[32,16,1024]{2,1,0:T(8,128)(2,1)}), bf16[32,16,1024]{2,1,0:T(8,128)(2,1)S(1)}, u32[]{:S(2)}, u32[]{:S(2)}) %all-to-all-start.1) | async-done | bytes 1048608 | tf_op jit(solution)/shard_map/all_to_all | solution.py:51
  47.3 5.6 %all-to-all-start = ((bf16[32,16,1024]{2,1,0:T(8,128)(2,1)}), bf16[32,16,1024]{2,1,0:T(8,128)(2,1)}, u32[]{:S(2)}, u32[]{:S(2)}) async-start(bf16[32,16,1024]{2,1,0:T(8,128)(2,1)} %bitcast.4), calls=%async_computation | async-start | bytes 2097152 | tf_op jit(solution)/shard_map/all_to_all | solution.py:52
  53.0 2.1 %fusion.2 = f32[512,768]{1,0:T(8,128)} fusion(bf16[512,1024]{1,0:T(8,128)(2,1)S(1)} %bitcast.54, bf16[1,1024,768]{2,1,0:T(8,128)(2,1)S(1)} %copy-done), kind=kOutput, calls=%fused_computation.9 | convolution fusion | flops 805306368 | bytes 4194304 | tf_op jit(solution)/shard_map/erd,edf->erf/dot_general | solution.py:12
  55.1 2.1 %fusion.5 = f32[512,768]{1,0:T(8,128)} fusion(bf16[512,1024]{1,0:T(8,128)(2,1)S(1)} %bitcast.55, bf16[1,1024,768]{2,1,0:T(8,128)(2,1)S(1)} %copy-done.2), kind=kOutput, calls=%fused_computation.12 | convolution fusion | flops 805306368 | bytes 4194304 | tf_op jit(solution)/shard_map/erd,edf->erf/dot_general | solution.py:13
  57.3 22.7 %all-to-all-done = bf16[32,16,1024]{2,1,0:T(8,128)(2,1)} async-done(((bf16[32,16,1024]{2,1,0:T(8,128)(2,1)}), bf16[32,16,1024]{2,1,0:T(8,128)(2,1)}, u32[]{:S(2)}, u32[]{:S(2)}) %all-to-all-start) | async-done | bytes 1048608 | tf_op jit(solution)/shard_map/all_to_all | solution.py:52
  80.0 4.1 %multiply_reduce_fusion = (bf16[512]{0:T(512)(128)(2,1)S(1)}, f32[512,768]{1,0:T(8,128)S(1)}) fusion(f32[512,768]{1,0:T(8,128)} %fusion.5, f32[512,768]{1,0:T(8,128)} %fusion.2, bf16[512,1024]{1,0:T(8,128)(2,1)} %bitcast.5, bf16[1,768,1024]{2,1,0:T(8,128)(2,1)} %param.13), kind=kOutput, calls=%fused_computation.16 | convolution fusion | flops 808058368 | bytes 7341056 | tf_op jit(solution)/shard_map/erd,efd->erf/dot_general | solution.py:21
  84.1 2.8 %fusion = f32[512,1024]{1,0:T(8,128)} fusion(bf16[1,1024,768]{2,1,0:T(8,128)(2,1)S(1)} %copy-done, f32[512,768]{1,0:T(8,128)S(1)} %copy-done.4, f32[512,768]{1,0:T(8,128)S(1)} %get-tuple-element.9, f32[512,768]{1,0:T(8,128)S(1)} %copy-done.5), kind=kOutput, calls=%fused_computation.7 | convolution fusion | flops 809238528 | bytes 8388608 | tf_op jit(solution)/shard_map/erf,edf->erd/dot_general | solution.py:27
  86.9 0.7 convert_element_type.54
  87.6 5.6 %all-to-all-start.3 = ((bf16[1,32,16]{2,0,1:T(2,128)(2,1)}), bf16[1,32,16]{2,0,1:T(2,128)(2,1)S(1)}, u32[]{:S(2)}, u32[]{:S(2)}) async-start(bf16[1,32,16]{2,0,1:T(2,128)(2,1)} %convert_element_type.54), calls=%async_computation.3 | async-start | bytes 32768 | tf_op jit(solution)/shard_map/all_to_all | solution.py:58
  93.2 3.6 %fusion.10 = bf16[1,512,1024]{2,1,0:T(8,128)(2,1)S(1)} fusion(f32[512,1024]{1,0:T(8,128)} %fusion, bf16[1,1024,768]{2,1,0:T(8,128)(2,1)S(1)} %copy-done.3, f32[512,768]{1,0:T(8,128)} %copy-done.6, f32[512,768]{1,0:T(8,128)} %fusion.2), kind=kOutput, calls=%fused_computation.21 | convolution fusion | flops 808714240 | bytes 7864320 | tf_op jit(solution)/shard_map/erf,edf->erd/dot_general | solution.py:28
  96.8 3.0 %copy.38 = bf16[1,512,1024]{2,0,1:T(2,128)(2,1)} copy(bf16[1,512,1024]{2,1,0:T(8,128)(2,1)S(1)} %fusion.10) | data formatting | bytes 2097152 | tf_op jit(solution)/shard_map/convert_element_type | solution.py:31
  100.3 8.0 %reduce.5 = bf16[512,1024]{1,0:T(8,128)(2,1)S(1)} reduce(bf16[512,1,1024]{2,1,0:T(2,128)(2,1)} %bitcast.53, bf16[]{:T(256)} %broadcast.163), dimensions={1}, to_apply=%bitcast.50.reduce_sub_computation | reduce | bytes 2097154
  108.3 1.6 %reshape.268 = bf16[32,2,8192]{2,1,0:T(2,128)(2,1)} reshape(bf16[512,1024]{1,0:T(8,128)(2,1)S(1)} %reduce.5) | data formatting | bytes 2097152
  109.9 9.9 %all-to-all-start.2 = ((bf16[32,2,8192]{2,1,0:T(2,128)(2,1)}), bf16[32,2,8192]{2,1,0:T(2,128)(2,1)S(1)}, u32[]{:S(2)}, u32[]{:S(2)}) async-start(bf16[32,2,8192]{2,1,0:T(2,128)(2,1)} %reshape.268), calls=%async_computation.2 | async-start | bytes 2097152 | tf_op jit(solution)/shard_map/all_to_all | solution.py:57
  120.1 1.9 %gather_fusion.1 = bf16[256]{0:T(256)(128)(2,1)S(1)} fusion(bf16[512]{0:T(512)(128)(2,1)S(1)} %reshape.203, s32[1024]{0:T(1024)S(1)} %pad_clamp_fusion), kind=kCustom, calls=%fused_computation.3 | custom fusion | bytes 2048 | tf_op jit(solution)/shard_map/gather | solution.py:64
  122.8 23.0 %all-to-all-done.2 = bf16[32,2,8192]{2,1,0:T(2,128)(2,1)S(1)} async-done(((bf16[32,2,8192]{2,1,0:T(2,128)(2,1)}), bf16[32,2,8192]{2,1,0:T(2,128)(2,1)S(1)}, u32[]{:S(2)}, u32[]{:S(2)}) %all-to-all-start.2) | async-done | bytes 1048608 | tf_op jit(solution)/shard_map/all_to_all | solution.py:57
  145.8 3.5 %reshape.269 = bf16[512,1,1024]{2,1,0:T(2,128)(2,1)} reshape(bf16[32,2,8192]{2,1,0:T(2,128)(2,1)S(1)} %all-to-all-done.2) | data formatting | bytes 2097152
  149.3 2.0 %copy.37 = bf16[1,512,1024]{2,1,0:T(8,128)(2,1)S(1)} copy(bf16[1,512,1024]{2,0,1:T(2,128)(2,1)} %bitcast.52) | data formatting | bytes 2097152
  151.2 1.2 gather_fusion
  153.0 2.1 %multiply_reduce_fusion.1 = bf16[128,1024]{1,0:T(8,128)(2,1)} fusion(f32[128,2,1024]{2,1,0:T(2,128)S(1)} %reshape.205, f32[128,2]{1,0:T(8,128)S(1)} %copy.29), kind=kLoop, calls=%fused_computation.23 | loop fusion | flops 393216 | bytes 1311744 | tf_op jit(solution)/shard_map/reduce_sum | solution.py:61
  (37 shorter events, 4.4 us)
Async XLA Ops:
  0.6 52.3 %copy-start = (bf16[1,1024,768]{2,1,0:T(8,128)(2,1)S(1)}, bf16[1,1024,768]{2,1,0:T(8,128)(2,1)}, u32[]{:S(2)}) copy-start(bf16[1,1024,768]{2,1,0:T(8,128)(2,1)} %param.11) | copy-start | bytes 4718596
  9.0 38.3 %all-to-all-start.1 = ((bf16[32,16,1024]{2,1,0:T(8,128)(2,1)}), bf16[32,16,1024]{2,1,0:T(8,128)(2,1)S(1)}, u32[]{:S(2)}, u32[]{:S(2)}) async-start(bf16[32,16,1024]{2,1,0:T(8,128)(2,1)} %bitcast.7), calls=%async_computation.1 | async-start | bytes 2097152 | tf_op jit(solution)/shard_map/all_to_all | solution.py:51
  47.3 32.7 %all-to-all-start = ((bf16[32,16,1024]{2,1,0:T(8,128)(2,1)}), bf16[32,16,1024]{2,1,0:T(8,128)(2,1)}, u32[]{:S(2)}, u32[]{:S(2)}) async-start(bf16[32,16,1024]{2,1,0:T(8,128)(2,1)} %bitcast.4), calls=%async_computation | async-start | bytes 2097152 | tf_op jit(solution)/shard_map/all_to_all | solution.py:52
  53.0 2.2 %copy-start.2 = (bf16[1,1024,768]{2,1,0:T(8,128)(2,1)S(1)}, bf16[1,1024,768]{2,1,0:T(8,128)(2,1)}, u32[]{:S(2)}) copy-start(bf16[1,1024,768]{2,1,0:T(8,128)(2,1)} %param.12) | copy-start | bytes 4718596
  80.0 4.1 %copy-start.4 = (f32[512,768]{1,0:T(8,128)S(1)}, f32[512,768]{1,0:T(8,128)}, u32[]{:S(2)}) copy-start(f32[512,768]{1,0:T(8,128)} %fusion.2) | copy-start | bytes 4718596
  80.0 4.1 %copy-start.5 = (f32[512,768]{1,0:T(8,128)S(1)}, f32[512,768]{1,0:T(8,128)}, u32[]{:S(2)}) copy-start(f32[512,768]{1,0:T(8,128)} %fusion.5) | copy-start | bytes 4718596
  84.1 2.9 %copy-start.6 = (f32[512,768]{1,0:T(8,128)}, f32[512,768]{1,0:T(8,128)S(1)}, u32[]{:S(2)}) copy-start(f32[512,768]{1,0:T(8,128)S(1)} %get-tuple-element.9) | copy-start | bytes 4718596
  84.1 9.1 %copy-start.3 = (bf16[1,1024,768]{2,1,0:T(8,128)(2,1)S(1)}, bf16[1,1024,768]{2,1,0:T(8,128)(2,1)}, u32[]{:S(2)}) copy-start(bf16[1,1024,768]{2,1,0:T(8,128)(2,1)} %param.12) | copy-start | bytes 4718596
  87.6 22.3 %all-to-all-start.3 = ((bf16[1,32,16]{2,0,1:T(2,128)(2,1)}), bf16[1,32,16]{2,0,1:T(2,128)(2,1)S(1)}, u32[]{:S(2)}, u32[]{:S(2)}) async-start(bf16[1,32,16]{2,0,1:T(2,128)(2,1)} %convert_element_type.54), calls=%async_computation.3 | async-start | bytes 32768 | tf_op jit(solution)/shard_map/all_to_all | solution.py:58
  109.9 9.9 %copy-start.1 = (f32[128,2]{0,1:T(2,128)S(1)}, f32[128,2]{0,1:T(2,128)}, u32[]{:S(2)}) copy-start(f32[128,2]{0,1:T(2,128)} %param.9) | copy-start | bytes 3076
  109.9 35.9 %all-to-all-start.2 = ((bf16[32,2,8192]{2,1,0:T(2,128)(2,1)}), bf16[32,2,8192]{2,1,0:T(2,128)(2,1)S(1)}, u32[]{:S(2)}, u32[]{:S(2)}) async-start(bf16[32,2,8192]{2,1,0:T(2,128)(2,1)} %reshape.268), calls=%async_computation.2 | async-start | bytes 2097152 | tf_op jit(solution)/shard_map/all_to_all | solution.py:57
where the time goes:
time: 156 us; the launch traced here: 155 us
  waiting for transfers between devices  68.5 us (44%)
  starting transfers between devices  31.3 us (20%)
  local copies, waits for them, and re-layouts  28.1 us (18%)
  matrix products  14.7 us (9%)
  other arithmetic  11.6 us (7%)
    all_to_all x1, waiting for transfers between devices, per_device(): lax.all_to_all(input_rows, 'expert', split_axis=1, concat_axis=0, tiled=T...  23 us
    all_to_all x1, waiting for transfers between devices, per_device(): lax.all_to_all(stash_send, 'expert', split_axis=0, concat_axis=1, tiled=T...  22.8 us
    all_to_all x1, waiting for transfers between devices, per_device(): lax.all_to_all(grad_send, 'expert', split_axis=0, concat_axis=1, tiled=True)  22.7 us
    all_to_all x1, starting transfers between devices, per_device(): lax.all_to_all(stash_send, 'expert', split_axis=0, concat_axis=1, tiled=T...  10.2 us
    all_to_all x1, starting transfers between devices, per_device(): lax.all_to_all(input_rows, 'expert', split_axis=1, concat_axis=0, tiled=T...  9.92 us
    unnamed x21, local copies, waits for them, and re-layouts  9.19 us
    unnamed x1, other arithmetic  8.03 us
    all_to_all x1, starting transfers between devices, per_device(): lax.all_to_all(grad_send, 'expert', split_axis=0, concat_axis=1, tiled=True)  5.62 us
  transfers between devices with their start and end apart: 4, of which 3 were waited for; matrix products, arithmetic and copies ran while one was open for 19% of the time, Pallas kernels for 0%

commit v1 on v0

v1 whole, which is shorter than its diff:
```python
import functools

import jax
import jax.numpy as jnp
from jax import lax
from jax.experimental import pallas as pl
from jax.experimental.pallas import tpu as pltpu
from jax.sharding import PartitionSpec as P

EXPERTS = 32
TOPK = 2
MOST = 16
NX = 4
NY = 8
CHUNKS = 4
PER = EXPERTS // CHUNKS
MESH = pl.DeviceIdType.MESH
BF16 = jnp.bfloat16
F32 = jnp.float32


def dot(a, b):
    return lax.dot_general(a, b, (((1,), (0,)), ((), ())), preferred_element_type=F32)


def dot_t(a, b):
    return lax.dot_general(a, b, (((1,), (1,)), ((), ())), preferred_element_type=F32)


def dy_of(c, half):
    if half == 0:
        return 4 - c
    return jnp.where(c == 0, 0, 4 + c)


def kernel(
    hid_ref, grad_ref, probs_ref, ids_ref, wg_hbm, wu_hbm, wd_hbm,
    out_ref, pg_ref,
    send_buf, recv_buf, back_send, back_recv, pb_send, pb_recv, wg, wu, wd,
    w_sem, fs_sem, fr_sem, bs_sem, br_sem, ps_sem, pr_sem,
):
    me = lax.axis_index("expert")
    my_y, my_x = me // NX, me % NX
    tok, width = hid_ref.shape
    ff = wg.shape[1]
    rows = PER * MOST

    barrier = pltpu.get_barrier_semaphore()

    def greet(i, carry):
        pl.semaphore_signal(barrier, inc=1, device_id={"expert": (me + i) % EXPERTS}, device_id_type=MESH)
        return carry

    lax.fori_loop(1, EXPERTS, greet, 0)
    weights = [
        pltpu.make_async_copy(wg_hbm.at[0], wg, w_sem.at[0]),
        pltpu.make_async_copy(wu_hbm.at[0], wu, w_sem.at[1]),
        pltpu.make_async_copy(wd_hbm.at[0], wd, w_sem.at[2]),
    ]
    for copy in weights:
        copy.start()

    ids = ids_ref[...]
    id0, id1 = ids[:, 0:1], ids[:, 1:2]
    lane = lax.broadcasted_iota(jnp.int32, (tok, tok), 1)
    sub = lax.broadcasted_iota(jnp.int32, (tok, tok), 0)
    named = jnp.logical_or(lane == id0, lane == id1)
    before = dot((lane < sub).astype(BF16), named.astype(BF16))
    rank0 = jnp.sum(jnp.where(lane == id0, before, 0.0), axis=1, keepdims=True).astype(jnp.int32)
    rank1 = jnp.sum(jnp.where(lane == id1, before, 0.0), axis=1, keepdims=True).astype(jnp.int32)
    tgt0, tgt1 = id0 * MOST + rank0, id1 * MOST + rank1
    eye = lane == sub
    row0 = jnp.sum(jnp.where(eye, tgt0, 0), axis=0, keepdims=True)
    row1 = jnp.sum(jnp.where(eye, tgt1, 0), axis=0, keepdims=True)
    half_rows = NX * MOST

    def pack(c):
        s = lax.broadcasted_iota(jnp.int32, (rows, tok), 0)
        y_a, y_b = (my_y + dy_of(c, 0)) % NY, (my_y + dy_of(c, 1)) % NY
        slot = jnp.where(s < half_rows, s + y_a * half_rows, s - half_rows + y_b * half_rows)
        pick = jnp.logical_or(slot == row0, slot == row1).astype(BF16)
        at = pl.ds(pl.multiple_of(c * rows, rows), rows)
        send_buf[at, :width] = dot(pick, hid_ref[...]).astype(BF16)
        send_buf[at, width:] = dot(pick, grad_ref[...]).astype(BF16)

    def out_copy(c, half, dx):
        i = c * 2 + half
        y = (my_y + dy_of(c, half)) % NY
        x = (my_x + dx) % NX
        slot = i * NX + my_x
        return pltpu.make_async_remote_copy(
            src_ref=send_buf.at[pl.ds(pl.multiple_of((i * NX + x) * MOST, MOST), MOST)],
            dst_ref=recv_buf.at[pl.ds(pl.multiple_of(slot * MOST, MOST), MOST)],
            send_sem=fs_sem.at[i * NX + dx],
            recv_sem=fr_sem.at[i * NX + dx],
            device_id={"expert": y * NX + x},
            device_id_type=MESH,
        )

    def back_copies(c, half, dx):
        i = c * 2 + half
        y = (my_y - dy_of(c, half) + NY) % NY
        x = (my_x - dx + NX) % NX
        return (
            pltpu.make_async_remote_copy(
                src_ref=back_send.at[pl.ds(pl.multiple_of((i * NX + x) * MOST, MOST), MOST)],
                dst_ref=back_recv.at[pl.ds(pl.multiple_of(me * MOST, MOST), MOST)],
                send_sem=bs_sem.at[i * NX + dx],
                recv_sem=br_sem.at[i * NX + dx],
                device_id={"expert": y * NX + x},
                device_id_type=MESH,
            ),
            pltpu.make_async_remote_copy(
                src_ref=pb_send.at[c],
                dst_ref=pb_recv.at[me],
                send_sem=ps_sem.at[i * NX + dx],
                recv_sem=pr_sem.at[i * NX + dx],
                device_id={"expert": y * NX + x},
                device_id_type=MESH,
            ),
        )

    def each(c, act):
        for half in range(2):
            for dx in range(NX):
                if half == 1 and dx == 0:
                    pl.when(c > 0)(functools.partial(act, half, dx))
                else:
                    act(half, dx)

    pack(0)
    pl.semaphore_wait(barrier, EXPERTS - 1)

    def send(c, carry):
        pl.when(c > 0)(functools.partial(pack, c))
        each(c, lambda half, dx: out_copy(c, half, dx).start())
        return carry

    lax.fori_loop(0, CHUNKS, send, 0)
    own_in = pl.ds(pl.multiple_of((NX + my_x) * MOST, MOST), MOST)
    recv_buf[own_in] = send_buf[own_in]
    for copy in weights:
        copy.wait()

    tile = 256

    def work(c, carry):
        each(c, lambda half, dx: out_copy(c, half, dx).wait_recv())
        at = pl.ds(pl.multiple_of(c * rows, rows), rows)
        x, g = recv_buf[at, :width], recv_buf[at, width:]
        total = jnp.zeros((rows, width), F32)
        prob = jnp.zeros((rows, 1), F32)
        for f in range(0, ff, tile):
            gate_pre = dot(x, wg[:, f : f + tile])
            up_pre = dot(x, wu[:, f : f + tile])
            hidden_grad = dot_t(g, wd[f : f + tile, :])
            sig = jax.nn.sigmoid(gate_pre)
            silu = gate_pre * sig
            prob += jnp.sum(hidden_grad * (silu * up_pre), axis=1, keepdims=True)
            gate_grad = (hidden_grad * up_pre * sig * (1.0 + gate_pre * (1.0 - sig))).astype(BF16)
            up_grad = (hidden_grad * silu).astype(BF16)
            total += dot_t(gate_grad, wg[:, f : f + tile]) + dot_t(up_grad, wu[:, f : f + tile])
        back_send[at] = total.astype(BF16)
        pb_send[c] = jnp.sum(
            jnp.where(eye, prob.astype(BF16).astype(F32), 0.0), axis=0, keepdims=True
        )

        def reply(half, dx):
            for copy in back_copies(c, half, dx):
                copy.start()

        each(c, reply)
        return carry

    lax.fori_loop(0, CHUNKS, work, 0)
    own_back = pl.ds(pl.multiple_of(me * MOST, MOST), MOST)
    back_recv[own_back] = back_send[own_in]
    pb_recv[me] = pb_send[0]

    def finish(c, carry):
        def settle(half, dx):
            out_copy(c, half, dx).wait_send()
            for copy in back_copies(c, half, dx):
                copy.wait()

        each(c, settle)
        return carry

    lax.fori_loop(0, CHUNKS, finish, 0)

    wide = lax.broadcasted_iota(jnp.int32, (tok, EXPERTS * MOST), 1)
    probs = probs_ref[...]
    first = dot((wide == tgt0).astype(BF16), back_recv[...])
    second = dot((wide == tgt1).astype(BF16), back_recv[...])
    out_ref[...] = (first * probs[:, 0:1] + second * probs[:, 1:2]).astype(BF16)

    scores = pb_recv[...].reshape(EXPERTS, tok).astype(BF16)
    expert = lax.broadcasted_iota(jnp.int32, (tok, EXPERTS), 1)
    column = lax.broadcasted_iota(jnp.int32, (tok, TOPK), 1)
    made = []
    for ident, rank in ((id0, rank0), (id1, rank1)):
        mine = dot((expert == ident).astype(BF16), scores)
        dy = (ident // NX - my_y + NY) % NY
        half = jnp.where(jnp.logical_or(dy == 0, dy > 4), 1, 0)
        place = (half * NX + my_x) * MOST + rank
        made.append(jnp.sum(jnp.where(lane == place, mine, 0.0), axis=1, keepdims=True))
    pg_ref[...] = jnp.where(column == 0, made[0], made[1]).astype(BF16)


def per_device(hidden_in, out_grad, gate_probs, expert_ids, w_gate, w_up, w_down):
    tok, width = hidden_in.shape
    ff = w_gate.shape[2]
    slots = EXPERTS * MOST
    vmem = pl.BlockSpec(memory_space=pltpu.VMEM)
    hbm = pl.BlockSpec(memory_space=pl.ANY)
    return pl.pallas_call(
        kernel,
        out_shape=(
            jax.ShapeDtypeStruct((tok, width), BF16),
            jax.ShapeDtypeStruct((tok, TOPK), BF16),
        ),
        in_specs=[vmem, vmem, vmem, vmem, hbm, hbm, hbm],
        out_specs=(vmem, vmem),
        scratch_shapes=[
            pltpu.VMEM((slots, 2 * width), BF16),
            pltpu.VMEM((slots, 2 * width), BF16),
            pltpu.VMEM((slots, width), BF16),
            pltpu.VMEM((slots, width), BF16),
            pltpu.VMEM((CHUNKS, 1, tok), F32),
            pltpu.VMEM((EXPERTS, 1, tok), F32),
            pltpu.VMEM((width, ff), BF16),
            pltpu.VMEM((width, ff), BF16),
            pltpu.VMEM((ff, width), BF16),
            pltpu.SemaphoreType.DMA((3,)),
            pltpu.SemaphoreType.DMA((EXPERTS,)),
            pltpu.SemaphoreType.DMA((EXPERTS,)),
            pltpu.SemaphoreType.DMA((EXPERTS,)),
            pltpu.SemaphoreType.DMA((EXPERTS,)),
            pltpu.SemaphoreType.DMA((EXPERTS,)),
            pltpu.SemaphoreType.DMA((EXPERTS,)),
        ],
        compiler_params=pltpu.CompilerParams(
            collective_id=0, has_side_effects=True, vmem_limit_bytes=48 * 1024 * 1024
        ),
    )(hidden_in, out_grad, gate_probs, expert_ids, w_gate, w_up, w_down)


def solution(mesh):
    in_specs = (
        P(("group", "expert"), None),
        P(("group", "expert"), None),
        P(("group", "expert"), None),
        P(("group", "expert"), None),
        P("expert", None, None),
        P("expert", None, None),
        P("expert", None, None),
    )
    out_specs = (P(("group", "expert"), None), P(("group", "expert"), None))
    return jax.shard_map(
        per_device, mesh=mesh, in_specs=in_specs, out_specs=out_specs, check_vma=False
    )
```

time: 156 us -> 92.6 us (0.59)
  the two profiles are of different devices: /device:TPU:324 before, /device:TPU:512 now
where the time goes in v1:
time: 92.6 us; the launch traced here: 92.3 us
  Pallas kernels  82.7 us (89%)
  local copies, waits for them, and re-layouts  8.99 us (10%)
    pallas_call x1, Pallas kernels, per_device(): pl.pallas_call(kernel, out_shape=(jax.ShapeDtypeStruct((tok, width), BF16...  82.7 us
    unnamed x13, local copies, waits for them, and re-layouts  8.39 us

profile of v1, /device:TPU:512, one launch (start us, length us, event | category | flops | bytes accessed | tf_op | source)
XLA Modules:
  0.0 92.3 jit_solution(46961574714658888)
XLA Ops:
  0.6 0.8 copy.9.probs_ref
  1.4 0.8 copy.10.ids_ref
  2.2 0.0 copy-start
  2.2 1.4 %copy-done = bf16[1,1024,768]{2,1,0:T(8,128)(2,1)S(1)} copy-done((bf16[1,1024,768]{2,1,0:T(8,128)(2,1)S(1)}, bf16[1,1024,768]{2,1,0:T(8,128)(2,1)}, u32[]{:S(2)}) %copy-start) | copy-done | bytes 1572888
  3.6 0.0 copy-start.1
  3.6 1.4 %copy-done.1 = bf16[1,1024,768]{2,1,0:T(8,128)(2,1)S(1)} copy-done((bf16[1,1024,768]{2,1,0:T(8,128)(2,1)S(1)}, bf16[1,1024,768]{2,1,0:T(8,128)(2,1)}, u32[]{:S(2)}) %copy-start.1) | copy-done | bytes 1572888
  5.0 0.0 copy-start.2
  5.0 1.4 %copy-done.2 = bf16[1,768,1024]{2,1,0:T(8,128)(2,1)S(1)} copy-done((bf16[1,768,1024]{2,1,0:T(8,128)(2,1)S(1)}, bf16[1,768,1024]{2,1,0:T(8,128)(2,1)}, u32[]{:S(2)}) %copy-start.2) | copy-done | bytes 1572888
  6.4 0.0 copy-start.3
  6.4 0.9 %copy-done.3 = bf16[128,1024]{1,0:T(8,128)(2,1)S(1)} copy-done((bf16[128,1024]{1,0:T(8,128)(2,1)S(1)}, bf16[128,1024]{1,0:T(8,128)(2,1)}, u32[]{:S(2)}) %copy-start.3) | copy-done | bytes 262168
  7.4 0.0 copy-start.4
  7.4 0.9 %copy-done.4 = bf16[128,1024]{1,0:T(8,128)(2,1)S(1)} copy-done((bf16[128,1024]{1,0:T(8,128)(2,1)S(1)}, bf16[128,1024]{1,0:T(8,128)(2,1)}, u32[]{:S(2)}) %copy-start.4) | copy-done | bytes 262168
  8.3 82.7 %shard_map.86 = (bf16[128,1024]{1,0:T(8,128)(2,1)S(1)}, bf16[128,2]{1,0:T(8,128)(2,1)S(1)}) custom-call(bf16[128,1024]{1,0:T(8,128)(2,1)S(1)} %copy-done.3, bf16[128,1024]{1,0:T(8,128)(2,1)S(1)} %copy-done.4, f32[128,2]{1,0:T(8,128)S(1)} %copy.9.probs_ref, s32[128,2]{1,0:T(8,128)S(1)} %copy.10.ids_ref, bf16[1,1024,768]{2,1,0:T(8,128)(2,1)S(1)} %copy-done, ...), custom_call_target="tpu_custom_call" | custom-call | tf_op jit(solution)/shard_map/pallas_call | solution.py:216
  91.0 0.6 copy.11
  91.6 0.7 copy.13
Async XLA Ops:
  2.2 1.4 %copy-start = (bf16[1,1024,768]{2,1,0:T(8,128)(2,1)S(1)}, bf16[1,1024,768]{2,1,0:T(8,128)(2,1)}, u32[]{:S(2)}) copy-start(bf16[1,1024,768]{2,1,0:T(8,128)(2,1)} %wg_hbm.1) | copy-start | bytes 4718596
  3.6 1.4 %copy-start.1 = (bf16[1,1024,768]{2,1,0:T(8,128)(2,1)S(1)}, bf16[1,1024,768]{2,1,0:T(8,128)(2,1)}, u32[]{:S(2)}) copy-start(bf16[1,1024,768]{2,1,0:T(8,128)(2,1)} %wu_hbm.1) | copy-start | bytes 4718596
  5.0 1.4 %copy-start.2 = (bf16[1,768,1024]{2,1,0:T(8,128)(2,1)S(1)}, bf16[1,768,1024]{2,1,0:T(8,128)(2,1)}, u32[]{:S(2)}) copy-start(bf16[1,768,1024]{2,1,0:T(8,128)(2,1)} %wd_hbm.1) | copy-start | bytes 4718596
  6.4 0.9 %copy-start.3 = (bf16[128,1024]{1,0:T(8,128)(2,1)S(1)}, bf16[128,1024]{1,0:T(8,128)(2,1)}, u32[]{:S(2)}) copy-start(bf16[128,1024]{1,0:T(8,128)(2,1)} %hid_ref.1) | copy-start | bytes 786436
  7.4 0.9 %copy-start.4 = (bf16[128,1024]{1,0:T(8,128)(2,1)S(1)}, bf16[128,1024]{1,0:T(8,128)(2,1)}, u32[]{:S(2)}) copy-start(bf16[128,1024]{1,0:T(8,128)(2,1)} %grad_ref.1) | copy-start | bytes 786436

commit v2 on v1

--- a/solution.py
+++ b/solution.py
@@ -34,9 +34,9 @@
 
 
 def kernel(
-    hid_ref, grad_ref, probs_ref, ids_ref, wg_hbm, wu_hbm, wd_hbm,
+    hid_hbm, grad_hbm, probs_hbm, ids_hbm, wg_hbm, wu_hbm, wd_hbm,
     out_ref, pg_ref,
-    send_buf, recv_buf, back_send, back_recv, pb_send, pb_recv, wg, wu, wd,
+    hid_ref, grad_ref, probs_ref, ids_ref, send_buf, recv_buf, back_send, back_recv, pb_send, pb_recv, wg, wu, wd,
     w_sem, fs_sem, fr_sem, bs_sem, br_sem, ps_sem, pr_sem,
 ):
     me = lax.axis_index("expert")
@@ -52,26 +52,36 @@
         return carry
 
     lax.fori_loop(1, EXPERTS, greet, 0)
-    weights = [
-        pltpu.make_async_copy(wg_hbm.at[0], wg, w_sem.at[0]),
-        pltpu.make_async_copy(wu_hbm.at[0], wu, w_sem.at[1]),
-        pltpu.make_async_copy(wd_hbm.at[0], wd, w_sem.at[2]),
-    ]
-    for copy in weights:
+    ids_in, hid_in, grad_in, probs_in, *weights = (
+        pltpu.make_async_copy(ids_hbm, ids_ref, w_sem.at[0]),
+        pltpu.make_async_copy(hid_hbm, hid_ref, w_sem.at[1]),
+        pltpu.make_async_copy(grad_hbm, grad_ref, w_sem.at[2]),
+        pltpu.make_async_copy(probs_hbm, probs_ref, w_sem.at[3]),
+        pltpu.make_async_copy(wg_hbm.at[0], wg, w_sem.at[4]),
+        pltpu.make_async_copy(wu_hbm.at[0], wu, w_sem.at[5]),
+        pltpu.make_async_copy(wd_hbm.at[0], wd, w_sem.at[6]),
+    )
+    for copy in (ids_in, hid_in, grad_in, probs_in, *weights):
         copy.start()
 
+    ids_in.wait()
     ids = ids_ref[...]
-    id0, id1 = ids[:, 0:1], ids[:, 1:2]
+    id0, id1 = ids[0:1, :], ids[1:2, :]
     lane = lax.broadcasted_iota(jnp.int32, (tok, tok), 1)
     sub = lax.broadcasted_iota(jnp.int32, (tok, tok), 0)
-    named = jnp.logical_or(lane == id0, lane == id1)
-    before = dot((lane < sub).astype(BF16), named.astype(BF16))
-    rank0 = jnp.sum(jnp.where(lane == id0, before, 0.0), axis=1, keepdims=True).astype(jnp.int32)
-    rank1 = jnp.sum(jnp.where(lane == id1, before, 0.0), axis=1, keepdims=True).astype(jnp.int32)
-    tgt0, tgt1 = id0 * MOST + rank0, id1 * MOST + rank1
+    named = jnp.logical_or(sub == id0, sub == id1)
+    before = dot(named.astype(BF16), (sub < lane).astype(BF16))
+    rank0 = jnp.sum(jnp.where(sub == id0, before, 0.0), axis=0, keepdims=True).astype(jnp.int32)
+    rank1 = jnp.sum(jnp.where(sub == id1, before, 0.0), axis=0, keepdims=True).astype(jnp.int32)
+    row0, row1 = id0 * MOST + rank0, id1 * MOST + rank1
     eye = lane == sub
-    row0 = jnp.sum(jnp.where(eye, tgt0, 0), axis=0, keepdims=True)
-    row1 = jnp.sum(jnp.where(eye, tgt1, 0), axis=0, keepdims=True)
+
+    def column(row):
+        return jnp.sum(jnp.where(eye, row, jnp.zeros_like(row)), axis=1, keepdims=True)
+
+    def flat(col):
+        return jnp.sum(jnp.where(eye, col, jnp.zeros_like(col)), axis=0, keepdims=True)
+
     half_rows = NX * MOST
 
     def pack(c):
@@ -128,6 +138,8 @@
                 else:
                     act(half, dx)
 
+    hid_in.wait()
+    grad_in.wait()
     pack(0)
     pl.semaphore_wait(barrier, EXPERTS - 1)
 
@@ -161,9 +173,7 @@
             up_grad = (hidden_grad * silu).astype(BF16)
             total += dot_t(gate_grad, wg[:, f : f + tile]) + dot_t(up_grad, wu[:, f : f + tile])
         back_send[at] = total.astype(BF16)
-        pb_send[c] = jnp.sum(
-            jnp.where(eye, prob.astype(BF16).astype(F32), 0.0), axis=0, keepdims=True
-        )
+        pb_send[c] = flat(prob.astype(BF16).astype(F32))
 
         def reply(half, dx):
             for copy in back_copies(c, half, dx):
@@ -189,22 +199,21 @@
     lax.fori_loop(0, CHUNKS, finish, 0)
 
     wide = lax.broadcasted_iota(jnp.int32, (tok, EXPERTS * MOST), 1)
+    probs_in.wait()
     probs = probs_ref[...]
-    first = dot((wide == tgt0).astype(BF16), back_recv[...])
-    second = dot((wide == tgt1).astype(BF16), back_recv[...])
-    out_ref[...] = (first * probs[:, 0:1] + second * probs[:, 1:2]).astype(BF16)
+    first = dot((wide == column(row0)).astype(BF16), back_recv[...])
+    second = dot((wide == column(row1)).astype(BF16), back_recv[...])
+    out_ref[...] = (first * column(probs[0:1, :]) + second * column(probs[1:2, :])).astype(BF16)
 
     scores = pb_recv[...].reshape(EXPERTS, tok).astype(BF16)
     expert = lax.broadcasted_iota(jnp.int32, (tok, EXPERTS), 1)
-    column = lax.broadcasted_iota(jnp.int32, (tok, TOPK), 1)
-    made = []
-    for ident, rank in ((id0, rank0), (id1, rank1)):
-        mine = dot((expert == ident).astype(BF16), scores)
+    for k, (ident, rank) in enumerate(((id0, rank0), (id1, rank1))):
+        mine = dot((expert == column(ident)).astype(BF16), scores)
         dy = (ident // NX - my_y + NY) % NY
         half = jnp.where(jnp.logical_or(dy == 0, dy > 4), 1, 0)
         place = (half * NX + my_x) * MOST + rank
-        made.append(jnp.sum(jnp.where(lane == place, mine, 0.0), axis=1, keepdims=True))
-    pg_ref[...] = jnp.where(column == 0, made[0], made[1]).astype(BF16)
+        found = jnp.sum(jnp.where(lane == column(place), mine, 0.0), axis=1, keepdims=True)
+        pg_ref[k : k + 1, :] = flat(found).astype(BF16)
 
 
 def per_device(hidden_in, out_grad, gate_probs, expert_ids, w_gate, w_up, w_down):
@@ -212,16 +221,20 @@
     ff = w_gate.shape[2]
     slots = EXPERTS * MOST
     vmem = pl.BlockSpec(memory_space=pltpu.VMEM)
-    hbm = pl.BlockSpec(memory_space=pl.ANY)
-    return pl.pallas_call(
+    hbm = pl.BlockSpec(memory_space=pltpu.HBM)
+    input_grad, prob_grad = pl.pallas_call(
         kernel,
         out_shape=(
             jax.ShapeDtypeStruct((tok, width), BF16),
-            jax.ShapeDtypeStruct((tok, TOPK), BF16),
+            jax.ShapeDtypeStruct((TOPK, tok), BF16),
         ),
-        in_specs=[vmem, vmem, vmem, vmem, hbm, hbm, hbm],
+        in_specs=[hbm] * 7,
         out_specs=(vmem, vmem),
         scratch_shapes=[
+            pltpu.VMEM((tok, width), BF16),
+            pltpu.VMEM((tok, width), BF16),
+            pltpu.VMEM((TOPK, tok), F32),
+            pltpu.VMEM((TOPK, tok), jnp.int32),
             pltpu.VMEM((slots, 2 * width), BF16),
             pltpu.VMEM((slots, 2 * width), BF16),
             pltpu.VMEM((slots, width), BF16),
@@ -231,7 +244,7 @@
             pltpu.VMEM((width, ff), BF16),
             pltpu.VMEM((width, ff), BF16),
             pltpu.VMEM((ff, width), BF16),
-            pltpu.SemaphoreType.DMA((3,)),
+            pltpu.SemaphoreType.DMA((7,)),
             pltpu.SemaphoreType.DMA((EXPERTS,)),
             pltpu.SemaphoreType.DMA((EXPERTS,)),
             pltpu.SemaphoreType.DMA((EXPERTS,)),
@@ -240,9 +253,10 @@
             pltpu.SemaphoreType.DMA((EXPERTS,)),
         ],
         compiler_params=pltpu.CompilerParams(
-            collective_id=0, has_side_effects=True, vmem_limit_bytes=48 * 1024 * 1024
+            collective_id=0, has_side_effects=True, vmem_limit_bytes=64 * 1024 * 1024
         ),
-    )(hidden_in, out_grad, gate_probs, expert_ids, w_gate, w_up, w_down)
+    )(hidden_in, out_grad, gate_probs.T, expert_ids.T, w_gate, w_up, w_down)
+    return input_grad, prob_grad.T
 
 
 def solution(mesh):

time: 92.6 us -> 87.2 us (0.942)
  the two profiles are of different devices: /device:TPU:512 before, /device:TPU:328 now
where the time goes in v2:
time: 87.2 us; the launch traced here: 87 us
  Pallas kernels  83.6 us (96%)
  local copies, waits for them, and re-layouts  2.8 us (3%)
    pallas_call x1, Pallas kernels, per_device(): pl.pallas_call(kernel, out_shape=(jax.ShapeDtypeStruct((tok, width), BF16...  83.6 us
    unnamed x2, local copies, waits for them, and re-layouts  2.8 us

profile of v2, /device:TPU:328, one launch (start us, length us, event | category | flops | bytes accessed | tf_op | source)
XLA Modules:
  0.0 87.0 jit_solution(13892409789826979144)
XLA Ops:
  0.6 83.6 %shard_map.86 = (bf16[128,1024]{1,0:T(8,128)(2,1)}, bf16[2,128]{1,0:T(2,128)(2,1)}) custom-call(bf16[128,1024]{1,0:T(8,128)(2,1)} %hid_hbm.1, bf16[128,1024]{1,0:T(8,128)(2,1)} %grad_hbm.1, f32[2,128]{1,0:T(2,128)} %bitcast.3, s32[2,128]{1,0:T(2,128)} %bitcast.4, bf16[1,1024,768]{2,1,0:T(8,128)(2,1)} %wg_hbm.1, bf16[1,1024,768]{2,1,0:T(8,128)(2,1)} %wu_hbm.1, ...), custom_call_target="tpu_custom_call" | custom-call | tf_op jit(solution)/shard_map/pallas_call | solution.py:225
  84.2 1.7 %copy.11 = bf16[128,1024]{1,0:T(8,128)(2,1)} copy(bf16[128,1024]{1,0:T(8,128)(2,1)} %get-tuple-element.8) | data formatting | bytes 524288
  85.9 1.1 %copy.12 = bf16[128,2]{0,1:T(2,128)(2,1)} copy(bf16[128,2]{0,1:T(2,128)(2,1)} %bitcast.5) | data formatting | bytes 1024

commit v3 on v2

--- a/solution.py
+++ b/solution.py
@@ -36,14 +36,17 @@
 def kernel(
     hid_hbm, grad_hbm, probs_hbm, ids_hbm, wg_hbm, wu_hbm, wd_hbm,
     out_ref, pg_ref,
-    hid_ref, grad_ref, probs_ref, ids_ref, send_buf, recv_buf, back_send, back_recv, pb_send, pb_recv, wg, wu, wd,
-    w_sem, fs_sem, fr_sem, bs_sem, br_sem, ps_sem, pr_sem,
+    own_tok, probs_ref, ids_ref, near_tok, own_tgt, near_tgt, send_buf, recv_buf,
+    back_send, back_recv, pb_send, pb_recv, wg, wu, wd,
+    w_sem, ns_sem, nr_sem, fs_sem, fr_sem, bs_sem, br_sem, ps_sem, pr_sem,
 ):
     me = lax.axis_index("expert")
     my_y, my_x = me // NX, me % NX
-    tok, width = hid_ref.shape
+    tok, width = hid_hbm.shape
     ff = wg.shape[1]
     rows = PER * MOST
+    band = NX * MOST
+    reach = NY // 2 * band
 
     barrier = pltpu.get_barrier_semaphore()
 
@@ -51,11 +54,10 @@
         pl.semaphore_signal(barrier, inc=1, device_id={"expert": (me + i) % EXPERTS}, device_id_type=MESH)
         return carry
 
-    lax.fori_loop(1, EXPERTS, greet, 0)
     ids_in, hid_in, grad_in, probs_in, *weights = (
         pltpu.make_async_copy(ids_hbm, ids_ref, w_sem.at[0]),
-        pltpu.make_async_copy(hid_hbm, hid_ref, w_sem.at[1]),
-        pltpu.make_async_copy(grad_hbm, grad_ref, w_sem.at[2]),
+        pltpu.make_async_copy(hid_hbm, own_tok.at[0], w_sem.at[1]),
+        pltpu.make_async_copy(grad_hbm, own_tok.at[1], w_sem.at[2]),
         pltpu.make_async_copy(probs_hbm, probs_ref, w_sem.at[3]),
         pltpu.make_async_copy(wg_hbm.at[0], wg, w_sem.at[4]),
         pltpu.make_async_copy(wu_hbm.at[0], wu, w_sem.at[5]),
@@ -63,6 +65,7 @@
     )
     for copy in (ids_in, hid_in, grad_in, probs_in, *weights):
         copy.start()
+    lax.fori_loop(1, EXPERTS, greet, 0)
 
     ids_in.wait()
     ids = ids_ref[...]
@@ -74,6 +77,7 @@
     rank0 = jnp.sum(jnp.where(sub == id0, before, 0.0), axis=0, keepdims=True).astype(jnp.int32)
     rank1 = jnp.sum(jnp.where(sub == id1, before, 0.0), axis=0, keepdims=True).astype(jnp.int32)
     row0, row1 = id0 * MOST + rank0, id1 * MOST + rank1
+    own_tgt[...] = jnp.where(lax.broadcasted_iota(jnp.int32, own_tgt.shape, 0) == 0, row0, row1)
     eye = lane == sub
 
     def column(row):
@@ -82,30 +86,51 @@
     def flat(col):
         return jnp.sum(jnp.where(eye, col, jnp.zeros_like(col)), axis=0, keepdims=True)
 
-    half_rows = NX * MOST
-
-    def pack(c):
-        s = lax.broadcasted_iota(jnp.int32, (rows, tok), 0)
-        y_a, y_b = (my_y + dy_of(c, 0)) % NY, (my_y + dy_of(c, 1)) % NY
-        slot = jnp.where(s < half_rows, s + y_a * half_rows, s - half_rows + y_b * half_rows)
-        pick = jnp.logical_or(slot == row0, slot == row1).astype(BF16)
-        at = pl.ds(pl.multiple_of(c * rows, rows), rows)
-        send_buf[at, :width] = dot(pick, hid_ref[...]).astype(BF16)
-        send_buf[at, width:] = dot(pick, grad_ref[...]).astype(BF16)
-
-    def out_copy(c, half, dx):
+    def near_copy(side, what):
+        src = own_tgt if what == 2 else own_tok.at[what]
+        dst = near_tgt.at[side] if what == 2 else near_tok.at[side, what]
+        y = (my_y + (1, NY - 1)[side]) % NY
+        return pltpu.make_async_remote_copy(
+            src_ref=src,
+            dst_ref=dst,
+            send_sem=ns_sem.at[side, what],
+            recv_sem=nr_sem.at[side, what],
+            device_id={"expert": y * NX + my_x},
+            device_id_type=MESH,
+        )
+
+    def pack(tensor, source, tgt, base, first_y, step, count):
+        s = lax.broadcasted_iota(jnp.int32, (count, tok), 0)
+        slot = ((first_y + step * (s // band) + NY) % NY) * band + s % band
+        pick = jnp.logical_or(slot == tgt[0], slot == tgt[1]).astype(BF16)
+        send_buf[tensor, base : base + count, :] = dot(pick, source[...]).astype(BF16)
+
+    def out_copy(tensor, c, half, dx):
+        own = jnp.logical_and(c == 0, half == 1)
+        side = jnp.where(c == 0, dx // 2, half)
+        off = jnp.where(own, 0, 3 - c)
+        base = jnp.where(own, 2 * reach, side * reach + off * band)
+        y = (my_y + (1 - 2 * side) * off + NY) % NY
+        x = (my_x + dx) % NX
         i = c * 2 + half
-        y = (my_y + dy_of(c, half)) % NY
-        x = (my_x + dx) % NX
-        slot = i * NX + my_x
         return pltpu.make_async_remote_copy(
-            src_ref=send_buf.at[pl.ds(pl.multiple_of((i * NX + x) * MOST, MOST), MOST)],
-            dst_ref=recv_buf.at[pl.ds(pl.multiple_of(slot * MOST, MOST), MOST)],
-            send_sem=fs_sem.at[i * NX + dx],
-            recv_sem=fr_sem.at[i * NX + dx],
+            src_ref=send_buf.at[tensor, pl.ds(pl.multiple_of(base + x * MOST, MOST), MOST)],
+            dst_ref=recv_buf.at[tensor, pl.ds(pl.multiple_of((i * NX + my_x) * MOST, MOST), MOST)],
+            send_sem=fs_sem.at[tensor, i * NX + dx],
+            recv_sem=fr_sem.at[tensor, i * NX + dx],
             device_id={"expert": y * NX + x},
             device_id_type=MESH,
         )
+
+    def each_out(c, act):
+        for half in range(2):
+            for dx in range(NX):
+                if dx > 0:
+                    act(half, dx)
+                elif half == 0:
+                    pl.when(c < 3)(functools.partial(act, half, dx))
+                else:
+                    pl.when(jnp.logical_and(c > 0, c < 3))(functools.partial(act, half, dx))
 
     def back_copies(c, half, dx):
         i = c * 2 + half
@@ -130,7 +155,7 @@
             ),
         )
 
-    def each(c, act):
+    def each_back(c, act):
         for half in range(2):
             for dx in range(NX):
                 if half == 1 and dx == 0:
@@ -140,26 +165,43 @@
 
     hid_in.wait()
     grad_in.wait()
-    pack(0)
     pl.semaphore_wait(barrier, EXPERTS - 1)
-
-    def send(c, carry):
-        pl.when(c > 0)(functools.partial(pack, c))
-        each(c, lambda half, dx: out_copy(c, half, dx).start())
-        return carry
-
-    lax.fori_loop(0, CHUNKS, send, 0)
-    own_in = pl.ds(pl.multiple_of((NX + my_x) * MOST, MOST), MOST)
-    recv_buf[own_in] = send_buf[own_in]
+    for what in (2, 0, 1):
+        for side in range(2):
+            near_copy(side, what).start()
+
+    for tensor in range(2):
+        pack(tensor, own_tok.at[tensor], (row0, row1), 2 * reach, my_y, 1, band)
+    for tensor in range(2):
+        for side in range(2):
+            if tensor == 0:
+                near_copy(side, 2).wait_recv()
+            near_copy(side, tensor).wait_recv()
+            tgt = near_tgt[side]
+            pack(
+                tensor, near_tok.at[side, tensor], (tgt[0:1, :], tgt[1:2, :]), side * reach, my_y, 1 - 2 * side, reach
+            )
+
+        def send(c, carry):
+            each_out(c, lambda half, dx: out_copy(tensor, c, half, dx).start())
+            return carry
+
+        lax.fori_loop(0, CHUNKS, send, 0)
+        for i, base in ((1, 2 * reach), (6, 0), (7, reach)):
+            into = pl.ds(pl.multiple_of((i * NX + my_x) * MOST, MOST), MOST)
+            out_of = pl.ds(pl.multiple_of(base + my_x * MOST, MOST), MOST)
+            recv_buf[tensor, into] = send_buf[tensor, out_of]
     for copy in weights:
         copy.wait()
 
     tile = 256
 
-    def work(c, carry):
-        each(c, lambda half, dx: out_copy(c, half, dx).wait_recv())
+    def work(turn, carry):
+        c = (turn + 3) % CHUNKS
+        for tensor in range(2):
+            each_out(c, lambda half, dx: out_copy(tensor, c, half, dx).wait_recv())
         at = pl.ds(pl.multiple_of(c * rows, rows), rows)
-        x, g = recv_buf[at, :width], recv_buf[at, width:]
+        x, g = recv_buf[0, at], recv_buf[1, at]
         total = jnp.zeros((rows, width), F32)
         prob = jnp.zeros((rows, 1), F32)
         for f in range(0, ff, tile):
@@ -179,24 +221,29 @@
             for copy in back_copies(c, half, dx):
                 copy.start()
 
-        each(c, reply)
+        each_back(c, reply)
         return carry
 
     lax.fori_loop(0, CHUNKS, work, 0)
     own_back = pl.ds(pl.multiple_of(me * MOST, MOST), MOST)
-    back_recv[own_back] = back_send[own_in]
+    back_recv[own_back] = back_send[pl.ds(pl.multiple_of((NX + my_x) * MOST, MOST), MOST)]
     pb_recv[me] = pb_send[0]
 
     def finish(c, carry):
+        for tensor in range(2):
+            each_out(c, lambda half, dx: out_copy(tensor, c, half, dx).wait_send())
+
         def settle(half, dx):
-            out_copy(c, half, dx).wait_send()
             for copy in back_copies(c, half, dx):
                 copy.wait()
 
-        each(c, settle)
+        each_back(c, settle)
         return carry
 
     lax.fori_loop(0, CHUNKS, finish, 0)
+    for what in range(3):
+        for side in range(2):
+            near_copy(side, what).wait_send()
 
     wide = lax.broadcasted_iota(jnp.int32, (tok, EXPERTS * MOST), 1)
     probs_in.wait()
@@ -231,12 +278,14 @@
         in_specs=[hbm] * 7,
         out_specs=(vmem, vmem),
         scratch_shapes=[
-            pltpu.VMEM((tok, width), BF16),
-            pltpu.VMEM((tok, width), BF16),
+            pltpu.VMEM((2, tok, width), BF16),
             pltpu.VMEM((TOPK, tok), F32),
             pltpu.VMEM((TOPK, tok), jnp.int32),
-            pltpu.VMEM((slots, 2 * width), BF16),
-            pltpu.VMEM((slots, 2 * width), BF16),
+            pltpu.VMEM((2, 2, tok, width), BF16),
+            pltpu.VMEM((8, tok), jnp.int32),
+            pltpu.VMEM((2, 8, tok), jnp.int32),
+            pltpu.VMEM((2, slots + NX * MOST, width), BF16),
+            pltpu.VMEM((2, slots, width), BF16),
             pltpu.VMEM((slots, width), BF16),
             pltpu.VMEM((slots, width), BF16),
             pltpu.VMEM((CHUNKS, 1, tok), F32),
@@ -245,8 +294,10 @@
             pltpu.VMEM((width, ff), BF16),
             pltpu.VMEM((ff, width), BF16),
             pltpu.SemaphoreType.DMA((7,)),
-            pltpu.SemaphoreType.DMA((EXPERTS,)),
-            pltpu.SemaphoreType.DMA((EXPERTS,)),
+            pltpu.SemaphoreType.DMA((2, 3)),
+            pltpu.SemaphoreType.DMA((2, 3)),
+            pltpu.SemaphoreType.DMA((2, EXPERTS)),
+            pltpu.SemaphoreType.DMA((2, EXPERTS)),
             pltpu.SemaphoreType.DMA((EXPERTS,)),
             pltpu.SemaphoreType.DMA((EXPERTS,)),
             pltpu.SemaphoreType.DMA((EXPERTS,)),

time: 87.2 us -> 78.4 us (0.90)
  the two profiles are of different devices: /device:TPU:328 before, /device:TPU:384 now
where the time goes in v3:
time: 78.4 us; the launch traced here: 78.2 us
  Pallas kernels  74.8 us (95%)
  local copies, waits for them, and re-layouts  2.8 us (4%)
    pallas_call x1, Pallas kernels, per_device(): pl.pallas_call(kernel, out_shape=(jax.ShapeDtypeStruct((tok, width), BF16...  74.8 us
    unnamed x2, local copies, waits for them, and re-layouts  2.8 us

profile of v3, /device:TPU:384, one launch (start us, length us, event | category | flops | bytes accessed | tf_op | source)
XLA Modules:
  0.0 78.2 jit_solution(9666382001178582747)
XLA Ops:
  0.6 74.8 %shard_map.86 = (bf16[128,1024]{1,0:T(8,128)(2,1)}, bf16[2,128]{1,0:T(2,128)(2,1)}) custom-call(bf16[128,1024]{1,0:T(8,128)(2,1)} %hid_hbm.1, bf16[128,1024]{1,0:T(8,128)(2,1)} %grad_hbm.1, f32[2,128]{1,0:T(2,128)} %bitcast.3, s32[2,128]{1,0:T(2,128)} %bitcast.4, bf16[1,1024,768]{2,1,0:T(8,128)(2,1)} %wg_hbm.1, bf16[1,1024,768]{2,1,0:T(8,128)(2,1)} %wu_hbm.1, ...), custom_call_target="tpu_custom_call" | custom-call | tf_op jit(solution)/shard_map/pallas_call | solution.py:272
  75.4 1.7 %copy.11 = bf16[128,1024]{1,0:T(8,128)(2,1)} copy(bf16[128,1024]{1,0:T(8,128)(2,1)} %get-tuple-element.8) | data formatting | bytes 524288
  77.1 1.1 %copy.12 = bf16[128,2]{0,1:T(2,128)(2,1)} copy(bf16[128,2]{0,1:T(2,128)(2,1)} %bitcast.5) | data formatting | bytes 1024

commit v4 on v3

--- a/solution.py
+++ b/solution.py
@@ -13,6 +13,7 @@
 NX = 4
 NY = 8
 CHUNKS = 4
+PARTS = 2
 PER = EXPERTS // CHUNKS
 MESH = pl.DeviceIdType.MESH
 BF16 = jnp.bfloat16
@@ -36,9 +37,9 @@
 def kernel(
     hid_hbm, grad_hbm, probs_hbm, ids_hbm, wg_hbm, wu_hbm, wd_hbm,
     out_ref, pg_ref,
-    own_tok, probs_ref, ids_ref, near_tok, own_tgt, near_tgt, send_buf, recv_buf,
-    back_send, back_recv, pb_send, pb_recv, wg, wu, wd,
-    w_sem, ns_sem, nr_sem, fs_sem, fr_sem, bs_sem, br_sem, ps_sem, pr_sem,
+    own_tok, probs_ref, ids_ref, near_tok, own_tgt, near_tgt, own_prob, near_prob, send_buf, recv_buf,
+    back_send, back_recv, part_send, part_recv, out_buf, pb_send, pb_recv, wg, wu, wd,
+    w_sem, ns_sem, nr_sem, fs_sem, fr_sem, bs_sem, br_sem, ps_sem, pr_sem, ts_sem, tr_sem, o_sem,
 ):
     me = lax.axis_index("expert")
     my_y, my_x = me // NX, me % NX
@@ -87,8 +88,8 @@
         return jnp.sum(jnp.where(eye, col, jnp.zeros_like(col)), axis=0, keepdims=True)
 
     def near_copy(side, what):
-        src = own_tgt if what == 2 else own_tok.at[what]
-        dst = near_tgt.at[side] if what == 2 else near_tok.at[side, what]
+        src = (own_tok.at[0], own_tok.at[1], own_tgt, own_prob)[what]
+        dst = (near_tok.at[side, 0], near_tok.at[side, 1], near_tgt.at[side], near_prob.at[side])[what]
         y = (my_y + (1, NY - 1)[side]) % NY
         return pltpu.make_async_remote_copy(
             src_ref=src,
@@ -99,18 +100,24 @@
             device_id_type=MESH,
         )
 
-    def pack(tensor, source, tgt, base, first_y, step, count):
-        s = lax.broadcasted_iota(jnp.int32, (count, tok), 0)
-        slot = ((first_y + step * (s // band) + NY) % NY) * band + s % band
+    def slots_of(shape, axis, step):
+        s = lax.broadcasted_iota(jnp.int32, shape, axis)
+        return ((my_y + step * (s // band) + NY) % NY) * band + s % band
+
+    def pack(tensor, source, tgt, base, step, count):
+        slot = slots_of((count, tok), 0, step)
         pick = jnp.logical_or(slot == tgt[0], slot == tgt[1]).astype(BF16)
         send_buf[tensor, base : base + count, :] = dot(pick, source[...]).astype(BF16)
 
-    def out_copy(tensor, c, half, dx):
+    def place_of(c, half, dx):
         own = jnp.logical_and(c == 0, half == 1)
         side = jnp.where(c == 0, dx // 2, half)
         off = jnp.where(own, 0, 3 - c)
-        base = jnp.where(own, 2 * reach, side * reach + off * band)
-        y = (my_y + (1 - 2 * side) * off + NY) % NY
+        return jnp.where(own, 2 * reach, side * reach + off * band), (1 - 2 * side) * off
+
+    def out_copy(tensor, c, half, dx):
+        base, off = place_of(c, half, dx)
+        y = (my_y + off + NY) % NY
         x = (my_x + dx) % NX
         i = c * 2 + half
         return pltpu.make_async_remote_copy(
@@ -132,27 +139,42 @@
                 else:
                     pl.when(jnp.logical_and(c > 0, c < 3))(functools.partial(act, half, dx))
 
-    def back_copies(c, half, dx):
+    def back_copy(c, half, dx):
+        base, off = place_of(c, half, dx)
+        i = c * 2 + half
+        y = (my_y - off + NY) % NY
+        x = (my_x - dx + NX) % NX
+        return pltpu.make_async_remote_copy(
+            src_ref=back_send.at[pl.ds(pl.multiple_of((i * NX + x) * MOST, MOST), MOST)],
+            dst_ref=back_recv.at[pl.ds(pl.multiple_of(base + my_x * MOST, MOST), MOST)],
+            send_sem=bs_sem.at[i * NX + dx],
+            recv_sem=br_sem.at[i * NX + dx],
+            device_id={"expert": y * NX + x},
+            device_id_type=MESH,
+        )
+
+    def prob_copy(c, half, dx):
         i = c * 2 + half
         y = (my_y - dy_of(c, half) + NY) % NY
         x = (my_x - dx + NX) % NX
-        return (
-            pltpu.make_async_remote_copy(
-                src_ref=back_send.at[pl.ds(pl.multiple_of((i * NX + x) * MOST, MOST), MOST)],
-                dst_ref=back_recv.at[pl.ds(pl.multiple_of(me * MOST, MOST), MOST)],
-                send_sem=bs_sem.at[i * NX + dx],
-                recv_sem=br_sem.at[i * NX + dx],
-                device_id={"expert": y * NX + x},
-                device_id_type=MESH,
-            ),
-            pltpu.make_async_remote_copy(
-                src_ref=pb_send.at[c],
-                dst_ref=pb_recv.at[me],
-                send_sem=ps_sem.at[i * NX + dx],
-                recv_sem=pr_sem.at[i * NX + dx],
-                device_id={"expert": y * NX + x},
-                device_id_type=MESH,
-            ),
+        return pltpu.make_async_remote_copy(
+            src_ref=pb_send.at[c],
+            dst_ref=pb_recv.at[me],
+            send_sem=ps_sem.at[i * NX + dx],
+            recv_sem=pr_sem.at[i * NX + dx],
+            device_id={"expert": y * NX + x},
+            device_id_type=MESH,
+        )
+
+    def part_copy(side, part):
+        y = (my_y + (NY - 1, 1)[side]) % NY
+        return pltpu.make_async_remote_copy(
+            src_ref=part_send.at[side, part],
+            dst_ref=part_recv.at[side, part],
+            send_sem=ts_sem.at[side, part],
+            recv_sem=tr_sem.at[side, part],
+            device_id={"expert": y * NX + my_x},
+            device_id_type=MESH,
         )
 
     def each_back(c, act):
@@ -163,15 +185,22 @@
                 else:
                     act(half, dx)
 
+    probs_in.wait()
+    probs = probs_ref[...]
+    own_prob[...] = jnp.where(
+        lax.broadcasted_iota(jnp.int32, own_prob.shape, 0) == 0, probs[0:1, :], probs[1:2, :]
+    )
+    for side in range(2):
+        back_recv[side * reach + 3 * band : (side + 1) * reach, :] = jnp.zeros((band, width), BF16)
     hid_in.wait()
     grad_in.wait()
     pl.semaphore_wait(barrier, EXPERTS - 1)
-    for what in (2, 0, 1):
+    for what in (2, 0, 1, 3):
         for side in range(2):
             near_copy(side, what).start()
 
     for tensor in range(2):
-        pack(tensor, own_tok.at[tensor], (row0, row1), 2 * reach, my_y, 1, band)
+        pack(tensor, own_tok.at[tensor], (row0, row1), 2 * reach, 1, band)
     for tensor in range(2):
         for side in range(2):
             if tensor == 0:
@@ -179,10 +208,11 @@
             near_copy(side, tensor).wait_recv()
             tgt = near_tgt[side]
             pack(
-                tensor, near_tok.at[side, tensor], (tgt[0:1, :], tgt[1:2, :]), side * reach, my_y, 1 - 2 * side, reach
+                tensor, near_tok.at[side, tensor], (tgt[0:1, :], tgt[1:2, :]), side * reach, 1 - 2 * side, reach
             )
 
-        def send(c, carry):
+        def send(turn, carry):
+            c = CHUNKS - 1 - turn
             each_out(c, lambda half, dx: out_copy(tensor, c, half, dx).start())
             return carry
 
@@ -197,7 +227,7 @@
     tile = 256
 
     def work(turn, carry):
-        c = (turn + 3) % CHUNKS
+        c = CHUNKS - 1 - turn
         for tensor in range(2):
             each_out(c, lambda half, dx: out_copy(tensor, c, half, dx).wait_recv())
         at = pl.ds(pl.multiple_of(c * rows, rows), rows)
@@ -217,40 +247,58 @@
         back_send[at] = total.astype(BF16)
         pb_send[c] = flat(prob.astype(BF16).astype(F32))
 
-        def reply(half, dx):
-            for copy in back_copies(c, half, dx):
-                copy.start()
-
-        each_back(c, reply)
+        each_out(c, lambda half, dx: back_copy(c, half, dx).start())
+        each_back(c, lambda half, dx: prob_copy(c, half, dx).start())
         return carry
 
     lax.fori_loop(0, CHUNKS, work, 0)
-    own_back = pl.ds(pl.multiple_of(me * MOST, MOST), MOST)
-    back_recv[own_back] = back_send[pl.ds(pl.multiple_of((NX + my_x) * MOST, MOST), MOST)]
+    for i, base in ((1, 2 * reach), (6, 0), (7, reach)):
+        into = pl.ds(pl.multiple_of(base + my_x * MOST, MOST), MOST)
+        back_recv[into] = back_send[pl.ds(pl.multiple_of((i * NX + my_x) * MOST, MOST), MOST)]
     pb_recv[me] = pb_send[0]
+
+    parts = part_send.shape[1]
+    span = width // parts
+    shares = []
+    for side in range(2):
+        near_copy(side, 3).wait_recv()
+        tgt, weight = near_tgt[side], near_prob[side]
+        slot = slots_of((tok, reach), 1, 1 - 2 * side)
+        shares.append(
+            [((slot == column(tgt[k : k + 1, :])).astype(BF16), column(weight[k : k + 1, :])) for k in range(TOPK)]
+        )
+    slot = slots_of((tok, band), 1, 1)
+    own_share = [
+        ((slot == column(row)).astype(BF16), column(probs[k : k + 1, :])) for k, row in enumerate((row0, row1))
+    ]
+
+    def summed(share, rows_ref):
+        (pick_a, weight_a), (pick_b, weight_b) = share
+        return dot(pick_a, rows_ref[...]) * weight_a + dot(pick_b, rows_ref[...]) * weight_b
+
+    def arrive(c, carry):
+        each_out(c, lambda half, dx: back_copy(c, half, dx).wait_recv())
+        return carry
+
+    lax.fori_loop(0, CHUNKS, arrive, 0)
+    for part in range(parts):
+        cols = slice(part * span, (part + 1) * span)
+        for side in range(2):
+            rows_ref = back_recv.at[side * reach : (side + 1) * reach, cols]
+            part_send[side, part] = summed(shares[side], rows_ref).astype(BF16)
+            part_copy(side, part).start()
 
     def finish(c, carry):
         for tensor in range(2):
             each_out(c, lambda half, dx: out_copy(tensor, c, half, dx).wait_send())
-
-        def settle(half, dx):
-            for copy in back_copies(c, half, dx):
-                copy.wait()
-
-        each_back(c, settle)
+        each_out(c, lambda half, dx: back_copy(c, half, dx).wait_send())
+        each_back(c, lambda half, dx: prob_copy(c, half, dx).wait())
         return carry
 
     lax.fori_loop(0, CHUNKS, finish, 0)
-    for what in range(3):
+    for what in range(4):
         for side in range(2):
             near_copy(side, what).wait_send()
-
-    wide = lax.broadcasted_iota(jnp.int32, (tok, EXPERTS * MOST), 1)
-    probs_in.wait()
-    probs = probs_ref[...]
-    first = dot((wide == column(row0)).astype(BF16), back_recv[...])
-    second = dot((wide == column(row1)).astype(BF16), back_recv[...])
-    out_ref[...] = (first * column(probs[0:1, :]) + second * column(probs[1:2, :])).astype(BF16)
 
     scores = pb_recv[...].reshape(EXPERTS, tok).astype(BF16)
     expert = lax.broadcasted_iota(jnp.int32, (tok, EXPERTS), 1)
@@ -261,6 +309,21 @@
         place = (half * NX + my_x) * MOST + rank
         found = jnp.sum(jnp.where(lane == column(place), mine, 0.0), axis=1, keepdims=True)
         pg_ref[k : k + 1, :] = flat(found).astype(BF16)
+
+    results = []
+    for part in range(parts):
+        cols = slice(part * span, (part + 1) * span)
+        own = summed(own_share, back_recv.at[2 * reach : 2 * reach + band, cols])
+        for side in range(2):
+            part_copy(side, part).wait_recv()
+        out_buf[part] = (own + part_recv[0, part].astype(F32) + part_recv[1, part].astype(F32)).astype(BF16)
+        results.append(pltpu.make_async_copy(out_buf.at[part], out_ref.at[:, cols], o_sem.at[part]))
+        results[-1].start()
+    for part in range(parts):
+        for side in range(2):
+            part_copy(side, part).wait_send()
+    for copy in results:
+        copy.wait()
 
 
 def per_device(hidden_in, out_grad, gate_probs, expert_ids, w_gate, w_up, w_down):
@@ -276,7 +339,7 @@
             jax.ShapeDtypeStruct((TOPK, tok), BF16),
         ),
         in_specs=[hbm] * 7,
-        out_specs=(vmem, vmem),
+        out_specs=(hbm, vmem),
         scratch_shapes=[
             pltpu.VMEM((2, tok, width), BF16),
             pltpu.VMEM((TOPK, tok), F32),
@@ -284,24 +347,32 @@
             pltpu.VMEM((2, 2, tok, width), BF16),
             pltpu.VMEM((8, tok), jnp.int32),
             pltpu.VMEM((2, 8, tok), jnp.int32),
+            pltpu.VMEM((8, tok), F32),
+            pltpu.VMEM((2, 8, tok), F32),
             pltpu.VMEM((2, slots + NX * MOST, width), BF16),
             pltpu.VMEM((2, slots, width), BF16),
             pltpu.VMEM((slots, width), BF16),
-            pltpu.VMEM((slots, width), BF16),
+            pltpu.VMEM((slots + NX * MOST, width), BF16),
+            pltpu.VMEM((2, PARTS, tok, width // PARTS), BF16),
+            pltpu.VMEM((2, PARTS, tok, width // PARTS), BF16),
+            pltpu.VMEM((PARTS, tok, width // PARTS), BF16),
             pltpu.VMEM((CHUNKS, 1, tok), F32),
             pltpu.VMEM((EXPERTS, 1, tok), F32),
             pltpu.VMEM((width, ff), BF16),
             pltpu.VMEM((width, ff), BF16),
             pltpu.VMEM((ff, width), BF16),
             pltpu.SemaphoreType.DMA((7,)),
-            pltpu.SemaphoreType.DMA((2, 3)),
-            pltpu.SemaphoreType.DMA((2, 3)),
+            pltpu.SemaphoreType.DMA((2, 4)),
+            pltpu.SemaphoreType.DMA((2, 4)),
             pltpu.SemaphoreType.DMA((2, EXPERTS)),
             pltpu.SemaphoreType.DMA((2, EXPERTS)),
             pltpu.SemaphoreType.DMA((EXPERTS,)),
             pltpu.SemaphoreType.DMA((EXPERTS,)),
             pltpu.SemaphoreType.DMA((EXPERTS,)),
             pltpu.SemaphoreType.DMA((EXPERTS,)),
+            pltpu.SemaphoreType.DMA((2, PARTS)),
+            pltpu.SemaphoreType.DMA((2, PARTS)),
+            pltpu.SemaphoreType.DMA((PARTS,)),
         ],
         compiler_params=pltpu.CompilerParams(
             collective_id=0, has_side_effects=True, vmem_limit_bytes=64 * 1024 * 1024

time: 78.4 us -> 81.2 us (1.036)
  the two profiles are of different devices: /device:TPU:384 before, /device:TPU:6 now
where the time goes in v4:
time: 81.2 us; the launch traced here: 81 us
  Pallas kernels  77.6 us (96%)
  local copies, waits for them, and re-layouts  2.8 us (3%)
    pallas_call x1, Pallas kernels, per_device(): pl.pallas_call(kernel, out_shape=(jax.ShapeDtypeStruct((tok, width), BF16...  77.6 us
    unnamed x2, local copies, waits for them, and re-layouts  2.8 us

profile of v4, /device:TPU:6, one launch (start us, length us, event | category | flops | bytes accessed | tf_op | source)
XLA Modules:
  0.0 81.0 jit_solution(5407968200931772702)
XLA Ops:
  0.6 77.6 %shard_map.86 = (bf16[128,1024]{1,0:T(8,128)(2,1)}, bf16[2,128]{1,0:T(2,128)(2,1)}) custom-call(bf16[128,1024]{1,0:T(8,128)(2,1)} %hid_hbm.1, bf16[128,1024]{1,0:T(8,128)(2,1)} %grad_hbm.1, f32[2,128]{1,0:T(2,128)} %bitcast.3, s32[2,128]{1,0:T(2,128)} %bitcast.4, bf16[1,1024,768]{2,1,0:T(8,128)(2,1)} %wg_hbm.1, bf16[1,1024,768]{2,1,0:T(8,128)(2,1)} %wu_hbm.1, ...), custom_call_target="tpu_custom_call" | custom-call | tf_op jit(solution)/shard_map/pallas_call | solution.py:335
  78.2 1.7 %copy.11 = bf16[128,1024]{1,0:T(8,128)(2,1)} copy(bf16[128,1024]{1,0:T(8,128)(2,1)} %get-tuple-element.8) | data formatting | bytes 524288
  79.9 1.1 %copy.12 = bf16[128,2]{0,1:T(2,128)(2,1)} copy(bf16[128,2]{0,1:T(2,128)(2,1)} %bitcast.5) | data formatting | bytes 1024

commit v5 on v4

--- a/solution.py
+++ b/solution.py
@@ -13,6 +13,7 @@
 NX = 4
 NY = 8
 CHUNKS = 4
+ROUNDS = NX // 2 + NY // 2 - 1
 PARTS = 2
 PER = EXPERTS // CHUNKS
 MESH = pl.DeviceIdType.MESH
@@ -39,7 +40,7 @@
     out_ref, pg_ref,
     own_tok, probs_ref, ids_ref, near_tok, own_tgt, near_tgt, own_prob, near_prob, send_buf, recv_buf,
     back_send, back_recv, part_send, part_recv, out_buf, pb_send, pb_recv, wg, wu, wd,
-    w_sem, ns_sem, nr_sem, fs_sem, fr_sem, bs_sem, br_sem, ps_sem, pr_sem, ts_sem, tr_sem, o_sem,
+    round_sem, w_sem, ns_sem, nr_sem, fs_sem, fr_sem, bs_sem, br_sem, ps_sem, pr_sem, ts_sem, tr_sem, o_sem,
 ):
     me = lax.axis_index("expert")
     my_y, my_x = me // NX, me % NX
@@ -51,9 +52,16 @@
 
     barrier = pltpu.get_barrier_semaphore()
 
-    def greet(i, carry):
-        pl.semaphore_signal(barrier, inc=1, device_id={"expert": (me + i) % EXPERTS}, device_id_type=MESH)
-        return carry
+    neighbours = (
+        (my_y + 1) % NY * NX + my_x,
+        (my_y + NY - 1) % NY * NX + my_x,
+        my_y * NX + (my_x + 1) % NX,
+        my_y * NX + (my_x + NX - 1) % NX,
+    )
+
+    def greet(sem):
+        for other in neighbours:
+            pl.semaphore_signal(sem, inc=1, device_id={"expert": other}, device_id_type=MESH)
 
     ids_in, hid_in, grad_in, probs_in, *weights = (
         pltpu.make_async_copy(ids_hbm, ids_ref, w_sem.at[0]),
@@ -66,7 +74,7 @@
     )
     for copy in (ids_in, hid_in, grad_in, probs_in, *weights):
         copy.start()
-    lax.fori_loop(1, EXPERTS, greet, 0)
+    greet(barrier)
 
     ids_in.wait()
     ids = ids_ref[...]
@@ -194,13 +202,16 @@
         back_recv[side * reach + 3 * band : (side + 1) * reach, :] = jnp.zeros((band, width), BF16)
     hid_in.wait()
     grad_in.wait()
-    pl.semaphore_wait(barrier, EXPERTS - 1)
+    pl.semaphore_wait(barrier, len(neighbours))
     for what in (2, 0, 1, 3):
         for side in range(2):
             near_copy(side, what).start()
 
     for tensor in range(2):
         pack(tensor, own_tok.at[tensor], (row0, row1), 2 * reach, 1, band)
+    for r in range(ROUNDS):
+        greet(round_sem.at[r])
+        pl.semaphore_wait(round_sem.at[r], len(neighbours))
     for tensor in range(2):
         for side in range(2):
             if tensor == 0:
@@ -212,7 +223,7 @@
             )
 
         def send(turn, carry):
-            c = CHUNKS - 1 - turn
+            c = turn
             each_out(c, lambda half, dx: out_copy(tensor, c, half, dx).start())
             return carry
 
@@ -227,7 +238,7 @@
     tile = 256
 
     def work(turn, carry):
-        c = CHUNKS - 1 - turn
+        c = (turn + 3) % CHUNKS
         for tensor in range(2):
             each_out(c, lambda half, dx: out_copy(tensor, c, half, dx).wait_recv())
         at = pl.ds(pl.multiple_of(c * rows, rows), rows)
@@ -361,6 +372,7 @@
             pltpu.VMEM((width, ff), BF16),
             pltpu.VMEM((width, ff), BF16),
             pltpu.VMEM((ff, width), BF16),
+            pltpu.SemaphoreType.REGULAR((ROUNDS,)),
             pltpu.SemaphoreType.DMA((7,)),
             pltpu.SemaphoreType.DMA((2, 4)),
             pltpu.SemaphoreType.DMA((2, 4)),

time: 81.2 us -> 76.9 us (0.947); the launches traced: 81 us -> 75.8 us
  Pallas kernels: 77.6 us -> 72.3 us
    pallas_call x1, Pallas kernels: 77.6 us -> 72.3 us  [per_device(): pl.pallas_call(kernel, out_shape=(jax.ShapeDtypeStruct((tok, width), BF16...]
where the time goes in v5:
time: 76.9 us; the launch traced here: 75.8 us
  Pallas kernels  72.3 us (94%)
  local copies, waits for them, and re-layouts  2.8 us (4%)
    pallas_call x1, Pallas kernels, per_device(): pl.pallas_call(kernel, out_shape=(jax.ShapeDtypeStruct((tok, width), BF16...  72.3 us
    unnamed x2, local copies, waits for them, and re-layouts  2.8 us

profile of v5, /device:TPU:6, one launch (start us, length us, event | category | flops | bytes accessed | tf_op | source)
XLA Modules:
  0.0 75.8 jit_solution(16702391788986674545)
XLA Ops:
  0.6 72.3 %shard_map.86 = (bf16[128,1024]{1,0:T(8,128)(2,1)}, bf16[2,128]{1,0:T(2,128)(2,1)}) custom-call(bf16[128,1024]{1,0:T(8,128)(2,1)} %hid_hbm.1, bf16[128,1024]{1,0:T(8,128)(2,1)} %grad_hbm.1, f32[2,128]{1,0:T(2,128)} %bitcast.3, s32[2,128]{1,0:T(2,128)} %bitcast.4, bf16[1,1024,768]{2,1,0:T(8,128)(2,1)} %wg_hbm.1, bf16[1,1024,768]{2,1,0:T(8,128)(2,1)} %wu_hbm.1, ...), custom_call_target="tpu_custom_call" | custom-call | tf_op jit(solution)/shard_map/pallas_call | solution.py:346
  73.0 1.7 %copy.11 = bf16[128,1024]{1,0:T(8,128)(2,1)} copy(bf16[128,1024]{1,0:T(8,128)(2,1)} %get-tuple-element.8) | data formatting | bytes 524288
  74.7 1.1 %copy.12 = bf16[128,2]{0,1:T(2,128)(2,1)} copy(bf16[128,2]{0,1:T(2,128)(2,1)} %bitcast.5) | data formatting | bytes 1024

commit v6 on v5

--- a/solution.py
+++ b/solution.py
@@ -13,8 +13,9 @@
 NX = 4
 NY = 8
 CHUNKS = 4
-ROUNDS = NX // 2 + NY // 2 - 1
+ROUNDS = 3
 PARTS = 2
+PIECES = 2
 PER = EXPERTS // CHUNKS
 MESH = pl.DeviceIdType.MESH
 BF16 = jnp.bfloat16
@@ -59,8 +60,14 @@
         my_y * NX + (my_x + NX - 1) % NX,
     )
 
-    def greet(sem):
-        for other in neighbours:
+    two_away = (
+        (my_y + 2) % NY * NX + my_x,
+        (my_y + NY - 2) % NY * NX + my_x,
+        my_y * NX + (my_x + 2) % NX,
+    )
+
+    def greet(sem, others):
+        for other in others:
             pl.semaphore_signal(sem, inc=1, device_id={"expert": other}, device_id_type=MESH)
 
     ids_in, hid_in, grad_in, probs_in, *weights = (
@@ -74,7 +81,7 @@
     )
     for copy in (ids_in, hid_in, grad_in, probs_in, *weights):
         copy.start()
-    greet(barrier)
+    greet(barrier, neighbours)
 
     ids_in.wait()
     ids = ids_ref[...]
@@ -209,9 +216,9 @@
 
     for tensor in range(2):
         pack(tensor, own_tok.at[tensor], (row0, row1), 2 * reach, 1, band)
-    for r in range(ROUNDS):
-        greet(round_sem.at[r])
-        pl.semaphore_wait(round_sem.at[r], len(neighbours))
+    for r, others in enumerate((neighbours, two_away, two_away)):
+        greet(round_sem.at[r], others)
+        pl.semaphore_wait(round_sem.at[r], len(others))
     for tensor in range(2):
         for side in range(2):
             if tensor == 0:
@@ -223,7 +230,7 @@
             )
 
         def send(turn, carry):
-            c = turn
+            c = (turn + 3) % CHUNKS
             each_out(c, lambda half, dx: out_copy(tensor, c, half, dx).start())
             return carry
 
@@ -335,6 +342,23 @@
             part_copy(side, part).wait_send()
     for copy in results:
         copy.wait()
+
+
+def deliver(grad_in, prob_in, grad_out, prob_out, grad_v, prob_v, in_sem, out_sem):
+    step = grad_v.shape[0] // PIECES
+    pieces = [(prob_in, prob_v, prob_out)]
+    for p in range(PIECES):
+        at = pl.ds(p * step, step)
+        pieces.append((grad_in.at[at], grad_v.at[at], grad_out.at[at]))
+    loads = [pltpu.make_async_copy(src, mid, in_sem.at[p]) for p, (src, mid, dst) in enumerate(pieces)]
+    stores = [pltpu.make_async_copy(mid, dst, out_sem.at[p]) for p, (src, mid, dst) in enumerate(pieces)]
+    for load in loads:
+        load.start()
+    for load, store in zip(loads, stores):
+        load.wait()
+        store.start()
+    for store in stores:
+        store.wait()
 
 
 def per_device(hidden_in, out_grad, gate_probs, expert_ids, w_gate, w_up, w_down):
@@ -390,6 +414,22 @@
             collective_id=0, has_side_effects=True, vmem_limit_bytes=64 * 1024 * 1024
         ),
     )(hidden_in, out_grad, gate_probs.T, expert_ids.T, w_gate, w_up, w_down)
+    input_grad, prob_grad = pl.pallas_call(
+        deliver,
+        out_shape=(
+            jax.ShapeDtypeStruct((tok, width), BF16),
+            jax.ShapeDtypeStruct((TOPK, tok), BF16),
+        ),
+        in_specs=[hbm] * 2,
+        out_specs=(hbm, hbm),
+        scratch_shapes=[
+            pltpu.VMEM((tok, width), BF16),
+            pltpu.VMEM((TOPK, tok), BF16),
+            pltpu.SemaphoreType.DMA((PIECES + 1,)),
+            pltpu.SemaphoreType.DMA((PIECES + 1,)),
+        ],
+        compiler_params=pltpu.CompilerParams(vmem_limit_bytes=64 * 1024 * 1024),
+    )(input_grad, prob_grad)
     return input_grad, prob_grad.T
 
 

time: 76.9 us -> 76.2 us (level); the launches traced: 75.8 us -> 76 us
  Pallas kernels: 72.3 us -> 75.4 us
  local copies, waits for them, and re-layouts: 2.8 us -> 0 us
    unnamed x2 -> x0, local copies, waits for them, and re-layouts: 2.8 us -> none
    pallas_call x0 -> x1, Pallas kernels: none -> 1.68 us  [per_device(): pl.pallas_call(deliver, out_shape=(jax.ShapeDtypeStruct((tok, width), BF1...]
    pallas_call x1, Pallas kernels: 72.3 us -> 73.7 us  [per_device(): pl.pallas_call(kernel, out_shape=(jax.ShapeDtypeStruct((tok, width), BF16...]
where the time goes in v6:
time: 76.2 us; the launch traced here: 76 us
  Pallas kernels  75.4 us (99%)
    pallas_call x1, Pallas kernels, per_device(): pl.pallas_call(kernel, out_shape=(jax.ShapeDtypeStruct((tok, width), BF16...  73.7 us
    pallas_call x1, Pallas kernels, per_device(): pl.pallas_call(deliver, out_shape=(jax.ShapeDtypeStruct((tok, width), BF1...  1.68 us

profile of v6, /device:TPU:6, one launch (start us, length us, event | category | flops | bytes accessed | tf_op | source)
XLA Modules:
  0.0 76.0 jit_solution(6568876254658247777)
XLA Ops:
  0.6 73.7 %shard_map.86 = (bf16[128,1024]{1,0:T(8,128)(2,1)}, bf16[2,128]{1,0:T(2,128)(2,1)}) custom-call(bf16[128,1024]{1,0:T(8,128)(2,1)} %hid_hbm.1, bf16[128,1024]{1,0:T(8,128)(2,1)} %grad_hbm.1, f32[2,128]{1,0:T(2,128)} %bitcast.3, s32[2,128]{1,0:T(2,128)} %bitcast.4, bf16[1,1024,768]{2,1,0:T(8,128)(2,1)} %wg_hbm.1, bf16[1,1024,768]{2,1,0:T(8,128)(2,1)} %wu_hbm.1, ...), custom_call_target="tpu_custom_call" | custom-call | tf_op jit(solution)/shard_map/pallas_call | solution.py:370
  74.4 1.7 %shard_map.87 = (bf16[128,1024]{1,0:T(8,128)(2,1)}, bf16[2,128]{1,0:T(2,128)(2,1)}) custom-call(bf16[128,1024]{1,0:T(8,128)(2,1)} %get-tuple-element.6.grad_in, bf16[2,128]{1,0:T(2,128)(2,1)} %get-tuple-element.7.prob_in), custom_call_target="tpu_custom_call" | custom-call | tf_op jit(solution)/shard_map/pallas_call | solution.py:417

commit v7 on v6

--- a/solution.py
+++ b/solution.py
@@ -230,7 +230,7 @@
             )
 
         def send(turn, carry):
-            c = (turn + 3) % CHUNKS
+            c = turn
             each_out(c, lambda half, dx: out_copy(tensor, c, half, dx).start())
             return carry
 

time: 76.2 us -> 75.6 us (level)
  Pallas kernels: 75.4 us -> 74.3 us
    pallas_call x1, Pallas kernels: 73.7 us -> 72.6 us  [per_device(): pl.pallas_call(kernel, out_shape=(jax.ShapeDtypeStruct((tok, width), BF16...]
where the time goes in v7:
time: 75.6 us; the launch traced here: 74.9 us
  Pallas kernels  74.3 us (98%)
    pallas_call x1, Pallas kernels, per_device(): pl.pallas_call(kernel, out_shape=(jax.ShapeDtypeStruct((tok, width), BF16...  72.6 us
    pallas_call x1, Pallas kernels, per_device(): pl.pallas_call(deliver, out_shape=(jax.ShapeDtypeStruct((tok, width), BF1...  1.68 us

profile of v7, /device:TPU:6, one launch (start us, length us, event | category | flops | bytes accessed | tf_op | source)
XLA Modules:
  0.0 74.9 jit_solution(2210841431059405750)
XLA Ops:
  0.6 72.6 %shard_map.86 = (bf16[128,1024]{1,0:T(8,128)(2,1)}, bf16[2,128]{1,0:T(2,128)(2,1)}) custom-call(bf16[128,1024]{1,0:T(8,128)(2,1)} %hid_hbm.1, bf16[128,1024]{1,0:T(8,128)(2,1)} %grad_hbm.1, f32[2,128]{1,0:T(2,128)} %bitcast.3, s32[2,128]{1,0:T(2,128)} %bitcast.4, bf16[1,1024,768]{2,1,0:T(8,128)(2,1)} %wg_hbm.1, bf16[1,1024,768]{2,1,0:T(8,128)(2,1)} %wu_hbm.1, ...), custom_call_target="tpu_custom_call" | custom-call | tf_op jit(solution)/shard_map/pallas_call | solution.py:370
  73.2 1.7 %shard_map.87 = (bf16[128,1024]{1,0:T(8,128)(2,1)}, bf16[2,128]{1,0:T(2,128)(2,1)}) custom-call(bf16[128,1024]{1,0:T(8,128)(2,1)} %get-tuple-element.6.grad_in, bf16[2,128]{1,0:T(2,128)(2,1)} %get-tuple-element.7.prob_in), custom_call_target="tpu_custom_call" | custom-call | tf_op jit(solution)/shard_map/pallas_call | solution.py:417

commit v8 on v7

--- a/solution.py
+++ b/solution.py
@@ -214,11 +214,11 @@
         for side in range(2):
             near_copy(side, what).start()
 
-    for tensor in range(2):
-        pack(tensor, own_tok.at[tensor], (row0, row1), 2 * reach, 1, band)
     for r, others in enumerate((neighbours, two_away, two_away)):
         greet(round_sem.at[r], others)
         pl.semaphore_wait(round_sem.at[r], len(others))
+    for tensor in range(2):
+        pack(tensor, own_tok.at[tensor], (row0, row1), 2 * reach, 1, band)
     for tensor in range(2):
         for side in range(2):
             if tensor == 0:

time: 75.6 us -> 75.6 us (level)
  no operation moved by 1% of the time
where the time goes in v8:
time: 75.6 us; the launch traced here: 75 us
  Pallas kernels  74.3 us (98%)
    pallas_call x1, Pallas kernels, per_device(): pl.pallas_call(kernel, out_shape=(jax.ShapeDtypeStruct((tok, width), BF16...  72.7 us
    pallas_call x1, Pallas kernels, per_device(): pl.pallas_call(deliver, out_shape=(jax.ShapeDtypeStruct((tok, width), BF1...  1.68 us

profile of v8, /device:TPU:6, one launch (start us, length us, event | category | flops | bytes accessed | tf_op | source)
XLA Modules:
  0.0 75.0 jit_solution(5912352286415688724)
XLA Ops:
  0.6 72.7 %shard_map.86 = (bf16[128,1024]{1,0:T(8,128)(2,1)}, bf16[2,128]{1,0:T(2,128)(2,1)}) custom-call(bf16[128,1024]{1,0:T(8,128)(2,1)} %hid_hbm.1, bf16[128,1024]{1,0:T(8,128)(2,1)} %grad_hbm.1, f32[2,128]{1,0:T(2,128)} %bitcast.3, s32[2,128]{1,0:T(2,128)} %bitcast.4, bf16[1,1024,768]{2,1,0:T(8,128)(2,1)} %wg_hbm.1, bf16[1,1024,768]{2,1,0:T(8,128)(2,1)} %wu_hbm.1, ...), custom_call_target="tpu_custom_call" | custom-call | tf_op jit(solution)/shard_map/pallas_call | solution.py:370
  73.3 1.7 %shard_map.87 = (bf16[128,1024]{1,0:T(8,128)(2,1)}, bf16[2,128]{1,0:T(2,128)(2,1)}) custom-call(bf16[128,1024]{1,0:T(8,128)(2,1)} %get-tuple-element.6.grad_in, bf16[2,128]{1,0:T(2,128)(2,1)} %get-tuple-element.7.prob_in), custom_call_target="tpu_custom_call" | custom-call | tf_op jit(solution)/shard_map/pallas_call | solution.py:417
